TPU v7x, 32 devices: a whole 2x2x4 slice. The times are simulated.
32 devices in a mesh: depth: 8 (over y, x, core), lat: 4 (over z).
Axes of the slice: x: 2, y: 2, z: 4, core: 2. Of those that a mesh axis runs over, the one named last changes fastest.
Arguments:
- rhs_field: float32 [2, 16, 8, 4096], P(None, 'depth', None, 'lat'), may hold values from -4 to 4
- src_cell: int32 [8], replicated, may hold values from 0 to 4095
- src_layer: int32 [8], replicated, may hold values from 0 to 15
- factor: float32 [16, 32, 3, 2, 128, 128], P('depth', 'lat'), as said below
- couple: float32 [2, 2, 16, 4096], P(None, None, 'depth', 'lat')
Outputs:
- waves: float32 [2, 16, 8, 4096], P(None, 'depth', None, 'lat')
- field: float32 [2, 16, 8, 4096], P(None, 'depth', None, 'lat')
Inputs may be any that keep to these rules, and one draw needn't show every extreme that they name: The centre block of every factor is a complex diagonal of modulus 0.92 plus independent entries; the others are independent entries.
All inputs are finite; a program needn't handle non-finite values.
Results may differ from a plain program's by a relative error of at most 0.0003.
Values sent between devices are 32-bit elements; how exact they have to be, the bound alone decides.
A program may use at most 128 MiB of HBM per device.

v0:
```python
import jax
import jax.numpy as jnp
from jax import lax
from jax.sharding import PartitionSpec as P


def extended(block, sides, width):
    for axis, dim in sides:
        count = lax.axis_size(axis)
        forward = [(i, i + 1) for i in range(count - 1)]
        backward = [(target, source) for source, target in forward]
        low = lax.ppermute(
            lax.slice_in_dim(block, block.shape[dim] - width, None, axis=dim), axis, forward
        )
        high = lax.ppermute(lax.slice_in_dim(block, 0, width, axis=dim), axis, backward)
        block = jnp.concatenate([low, block, high], axis=dim)
    return block


def from_behind(value, axis, steps):
    count = lax.axis_size(axis)
    leading, last = (max(0, -steps), min(count, count - steps))
    return lax.ppermute(value, axis, [(source, source + steps) for source in range(leading, last)])


def complex_scale(coef, vector):
    real_part = coef[0][None, :] * vector[0] - coef[1][None, :] * vector[1]
    imag_part = coef[0][None, :] * vector[1] + coef[1][None, :] * vector[0]
    return jnp.stack([real_part, imag_part])


def block_product(padded, blocks, strip_cells):
    tile_cells = blocks.shape[-1]
    tile_count = strip_cells // tile_cells
    shot_count = padded.shape[1]
    shifted = jnp.stack(
        [
            padded[:, :, offset * tile_cells : offset * tile_cells + strip_cells].reshape(
                2, shot_count, tile_count, tile_cells
            )
            for offset in range(3)
        ],
        axis=3,
    )
    form = "stjp,tjpq->stq"
    high = lax.Precision.HIGHEST
    real_out = jnp.einsum(form, shifted[0], blocks[:, :, 0], precision=high) - jnp.einsum(
        form, shifted[1], blocks[:, :, 1], precision=high
    )
    imag_out = jnp.einsum(form, shifted[0], blocks[:, :, 1], precision=high) + jnp.einsum(
        form, shifted[1], blocks[:, :, 0], precision=high
    )
    return jnp.stack([real_out, imag_out]).reshape(2, shot_count, strip_cells)


def apply_blocks(vector, blocks):
    tile_cells = blocks.shape[-1]
    padded = extended(vector, (("lat", 2),), tile_cells)
    return block_product(padded, blocks, vector.shape[-1])


def descend(batch_forcing, incoming, factor, couple_down, applier):
    carried = incoming
    wave_list = []
    for layer_num in range(batch_forcing.shape[1]):
        source = batch_forcing[:, layer_num] + complex_scale(couple_down[:, layer_num], carried)
        carried = applier(source, factor[layer_num])
        wave_list.append(carried)
    return (jnp.stack(wave_list, axis=1), carried)


def ascend(batch_waves, incoming, factor, couple_up, applier):
    carried = incoming
    layer_total = batch_waves.shape[1]
    field_list = [None] * layer_total
    for layer_num in reversed(range(layer_total)):
        carried = batch_waves[:, layer_num] + applier(
            complex_scale(couple_up[:, layer_num], carried), factor[layer_num]
        )
        field_list[layer_num] = carried
    return (jnp.stack(field_list, axis=1), carried)


def shards(rhs_field, src_cell, src_layer, factor, couple):
    layer_total = rhs_field.shape[1]
    shot_count = rhs_field.shape[2]
    strip_cells = rhs_field.shape[3]
    depth_pos = lax.axis_index("depth")
    lat_pos = lax.axis_index("lat")
    depth_count = lax.axis_size("depth")
    layer_ids = depth_pos * layer_total + jnp.arange(layer_total, dtype=jnp.int32)
    cell_ids = lat_pos * strip_cells + jnp.arange(strip_cells, dtype=jnp.int32)
    hit = (src_layer[None, :, None] == layer_ids[:, None, None]) & (
        src_cell[None, :, None] == cell_ids[None, None, :]
    )
    real_part = rhs_field[0] + 4.0 * hit.astype(jnp.float32)
    forcing = jnp.stack([real_part, rhs_field[1]])
    down_use = couple[0]
    up_use = couple[1]
    batch_count = 1
    batch_rows = shot_count // batch_count
    start_state = jnp.zeros((2, batch_rows, strip_cells), jnp.float32)
    segment_total = depth_count + batch_count - 1

    def down_segment(segment_num, carry):
        incoming, result = carry
        batch_num = segment_num - depth_pos
        active_flag = (batch_num >= 0) & (batch_num < batch_count)
        offset_rows = jnp.clip(batch_num, 0, batch_count - 1) * batch_rows
        wave_part, deepest = descend(forcing, incoming, factor, down_use, apply_blocks)
        updated = lax.dynamic_update_slice_in_dim(result, wave_part, offset_rows, 2)
        result = jnp.where(active_flag, updated, result)
        outgoing = from_behind(deepest, "depth", 1)
        return (outgoing, result)

    _, waves = lax.fori_loop(0, segment_total, down_segment, (start_state, jnp.zeros_like(forcing)))

    def up_segment(segment_num, carry):
        incoming, result = carry
        batch_num = segment_num - (depth_count - 1 - depth_pos)
        active_flag = (batch_num >= 0) & (batch_num < batch_count)
        offset_rows = jnp.clip(batch_num, 0, batch_count - 1) * batch_rows
        field_part, shallowest = ascend(waves, incoming, factor, up_use, apply_blocks)
        updated = lax.dynamic_update_slice_in_dim(result, field_part, offset_rows, 2)
        result = jnp.where(active_flag, updated, result)
        outgoing = from_behind(shallowest, "depth", -1)
        return (outgoing, result)

    _, field = lax.fori_loop(0, segment_total, up_segment, (start_state, jnp.zeros_like(forcing)))
    return (waves, field)


def solution(mesh):
    placed = (
        P(None, "depth", None, "lat"),
        P(),
        P(),
        P("depth", "lat", None, None, None, None),
        P(None, None, "depth", "lat"),
    )
    return jax.shard_map(
        shards,
        mesh=mesh,
        in_specs=placed,
        out_specs=(P(None, "depth", None, "lat"), P(None, "depth", None, "lat")),
        check_vma=False,
    )
```

profile of v0, /device:TPU:0, one launch (start us, length us, event | category | flops | bytes accessed | tf_op | source)
XLA Modules:
  0.0 552.9 jit_solution(6284804765796779296)
XLA Ops:
  3.9 6.2 %copy.13 = f32[2,8,3,2,128,128]{5,4,2,1,3,0:T(8,128)} copy(f32[2,8,3,2,128,128]{5,4,3,2,1,0:T(8,128)} %param.12) | data formatting | bytes 12582912
  10.7 274.8 %while.34 = (s32[]{:T(128)}, f32[2,8,1024]{2,1,0:T(8,128)S(1)}, f32[2,2,8,1024]{3,2,1,0:T(8,128)S(1)}, f32[2,2,8,1024]{3,2,0,1:T(8,128)S(1)}, f32[2,2,1024]{2,1,...) while((s32[]{:T(128)}, f32[2,8,1024]{2,1,0:T(8,128)S(1)}, ...), condition=%wide.region_1.2_spmd.clone, body=%wide.region_0.1_spmd.clone.sunk | while | flops 302743552 | bytes 48751040 | solution.py:116
  11.4 5.5 collective-permute-start
  28.3 4.5 collective-permute-start.2
  60.3 4.5 collective-permute-start.2
  66.3 4.2 collective-permute-done.3
  94.0 4.5 collective-permute-start.2
  108.2 4.7 collective-permute-start.4
  128.6 4.5 collective-permute-start.2
  142.8 4.4 collective-permute-start.4
  163.0 4.5 collective-permute-start.2
  177.2 4.4 collective-permute-start.4
  197.3 4.5 collective-permute-start.2
  211.5 4.4 collective-permute-start.4
  231.6 4.5 collective-permute-start.2
  245.9 4.4 collective-permute-start.4
  266.0 4.5 collective-permute-start.2
  280.2 4.4 collective-permute-start.4
  286.2 266.0 %while.35 = (s32[]{:T(128)}, f32[2,8,1024]{2,1,0:T(8,128)}, f32[2,2,8,1024]{3,2,1,0:T(8,128)S(1)}, f32[2,2,8,1024]{3,2,1,0:T(8,128)S(1)}, f32[2,2,1024]{2,1,0:T(...) while((s32[]{:T(128)}, f32[2,8,1024]{2,1,0:T(8,128)}, ...), condition=%wide.region_3.4_spmd.clone, body=%wide.region_2.3_spmd.clone.sunk | while | flops 302784512 | bytes 29606224 | solution.py:129
  305.2 4.3 collective-permute-done.8
  338.3 4.3 collective-permute-done.8
  348.9 5.1 collective-permute-done.9
  367.1 4.2 collective-permute-start.7
  372.6 4.3 collective-permute-done.8
  383.1 4.6 collective-permute-done.9
  400.8 4.2 collective-permute-start.7
  406.3 4.3 collective-permute-done.8
  416.9 5.8 %collective-permute-done.9 = f32[2,8,1024]{2,1,0:T(8,128)} collective-permute-done((f32[2,8,1024]{2,1,0:T(8,128)S(1)}, f32[2,8,1024]{2,1,0:T(8,128)}, u32[]{:S(2)}, u32[]{:S(2)}) %collective-permute-start.9) | collective-permute-done | bytes 65568 | tf_op jit(solution)/shard_map/while/body/eval_jaxpr/ppermute | solution.py:23
  441.3 4.3 collective-permute-done.8
  473.7 4.3 collective-permute-done.8
  506.0 4.3 collective-permute-done.8
  538.4 4.3 collective-permute-done.8
  (589 shorter events, 410.8 us)
Async XLA Ops:
  11.4 12.0 %collective-permute-start = (f32[2,8,128]{2,1,0:T(8,128)}, f32[2,8,128]{2,1,0:T(8,128)}, u32[]{:S(2)}, u32[]{:S(2)}) collective-permute-start(f32[2,8,128]{2,1,0:T(8,128)} %get-tuple-element.562), channel_id=1, source_target_pairs={{0,1},{1,2},{2,3},{4,5},{5,6},{6,7},{8,9},{9,10},{10,11},{12,13},{... | collective-permute-start | bytes 24584 | tf_op jit(solution)/shard_map/while/body/eval_jaxpr/ppermute | solution.py:12
  16.9 6.5 %collective-permute-start.1 = (f32[2,8,128]{2,1,0:T(8,128)S(1)}, f32[2,8,128]{2,1,0:T(8,128)}, u32[]{:S(2)}, u32[]{:S(2)}) collective-permute-start(f32[2,8,128]{2,1,0:T(8,128)S(1)} %get-tuple-element.563), channel_id=1, source_target_pairs={{1,0},{2,1},{3,2},{5,4},{6,5},{7,6},{9,8},{10,9},{11,10},{13,12},{... | collective-permute-start | bytes 24584 | tf_op jit(solution)/shard_map/while/body/eval_jaxpr/ppermute | solution.py:15
  28.3 5.9 %collective-permute-start.2 = (f32[2,8,128]{2,1,0:T(8,128)S(1)}, f32[2,8,128]{2,1,0:T(8,128)S(1)}, u32[]{:S(2)}, u32[]{:S(2)}) collective-permute-start(f32[2,8,128]{2,1,0:T(8,128)S(1)} %get-tuple-element.570), channel_id=1, source_target_pairs={{0,1},{1,2},{2,3},{4,5},{5,6},{6,7},{8,9},{9,10},{10,11},{12,13},{... | collective-permute-start | bytes 24584 | tf_op jit(solution)/shard_map/while/body/eval_jaxpr/ppermute | solution.py:12
  45.3 10.1 %collective-permute-start = (f32[2,8,128]{2,1,0:T(8,128)}, f32[2,8,128]{2,1,0:T(8,128)}, u32[]{:S(2)}, u32[]{:S(2)}) collective-permute-start(f32[2,8,128]{2,1,0:T(8,128)} %get-tuple-element.562), channel_id=1, source_target_pairs={{0,1},{1,2},{2,3},{4,5},{5,6},{6,7},{8,9},{9,10},{10,11},{12,13},{... | collective-permute-start | bytes 24584 | tf_op jit(solution)/shard_map/while/body/eval_jaxpr/ppermute | solution.py:12
  49.0 6.5 %collective-permute-start.1 = (f32[2,8,128]{2,1,0:T(8,128)S(1)}, f32[2,8,128]{2,1,0:T(8,128)}, u32[]{:S(2)}, u32[]{:S(2)}) collective-permute-start(f32[2,8,128]{2,1,0:T(8,128)S(1)} %get-tuple-element.563), channel_id=1, source_target_pairs={{1,0},{2,1},{3,2},{5,4},{6,5},{7,6},{9,8},{10,9},{11,10},{13,12},{... | collective-permute-start | bytes 24584 | tf_op jit(solution)/shard_map/while/body/eval_jaxpr/ppermute | solution.py:15
  60.3 5.9 %collective-permute-start.2 = (f32[2,8,128]{2,1,0:T(8,128)S(1)}, f32[2,8,128]{2,1,0:T(8,128)S(1)}, u32[]{:S(2)}, u32[]{:S(2)}) collective-permute-start(f32[2,8,128]{2,1,0:T(8,128)S(1)} %get-tuple-element.570), channel_id=1, source_target_pairs={{0,1},{1,2},{2,3},{4,5},{5,6},{6,7},{8,9},{9,10},{10,11},{12,13},{... | collective-permute-start | bytes 24584 | tf_op jit(solution)/shard_map/while/body/eval_jaxpr/ppermute | solution.py:12
  78.7 10.4 %collective-permute-start = (f32[2,8,128]{2,1,0:T(8,128)}, f32[2,8,128]{2,1,0:T(8,128)}, u32[]{:S(2)}, u32[]{:S(2)}) collective-permute-start(f32[2,8,128]{2,1,0:T(8,128)} %get-tuple-element.562), channel_id=1, source_target_pairs={{0,1},{1,2},{2,3},{4,5},{5,6},{6,7},{8,9},{9,10},{10,11},{12,13},{... | collective-permute-start | bytes 24584 | tf_op jit(solution)/shard_map/while/body/eval_jaxpr/ppermute | solution.py:12
  82.6 6.5 %collective-permute-start.1 = (f32[2,8,128]{2,1,0:T(8,128)S(1)}, f32[2,8,128]{2,1,0:T(8,128)}, u32[]{:S(2)}, u32[]{:S(2)}) collective-permute-start(f32[2,8,128]{2,1,0:T(8,128)S(1)} %get-tuple-element.563), channel_id=1, source_target_pairs={{1,0},{2,1},{3,2},{5,4},{6,5},{7,6},{9,8},{10,9},{11,10},{13,12},{... | collective-permute-start | bytes 24584 | tf_op jit(solution)/shard_map/while/body/eval_jaxpr/ppermute | solution.py:15
  94.0 5.9 %collective-permute-start.2 = (f32[2,8,128]{2,1,0:T(8,128)S(1)}, f32[2,8,128]{2,1,0:T(8,128)S(1)}, u32[]{:S(2)}, u32[]{:S(2)}) collective-permute-start(f32[2,8,128]{2,1,0:T(8,128)S(1)} %get-tuple-element.570), channel_id=1, source_target_pairs={{0,1},{1,2},{2,3},{4,5},{5,6},{6,7},{8,9},{9,10},{10,11},{12,13},{... | collective-permute-start | bytes 24584 | tf_op jit(solution)/shard_map/while/body/eval_jaxpr/ppermute | solution.py:12
  114.5 9.3 %collective-permute-start = (f32[2,8,128]{2,1,0:T(8,128)}, f32[2,8,128]{2,1,0:T(8,128)}, u32[]{:S(2)}, u32[]{:S(2)}) collective-permute-start(f32[2,8,128]{2,1,0:T(8,128)} %get-tuple-element.562), channel_id=1, source_target_pairs={{0,1},{1,2},{2,3},{4,5},{5,6},{6,7},{8,9},{9,10},{10,11},{12,13},{... | collective-permute-start | bytes 24584 | tf_op jit(solution)/shard_map/while/body/eval_jaxpr/ppermute | solution.py:12
  117.2 6.5 %collective-permute-start.1 = (f32[2,8,128]{2,1,0:T(8,128)S(1)}, f32[2,8,128]{2,1,0:T(8,128)}, u32[]{:S(2)}, u32[]{:S(2)}) collective-permute-start(f32[2,8,128]{2,1,0:T(8,128)S(1)} %get-tuple-element.563), channel_id=1, source_target_pairs={{1,0},{2,1},{3,2},{5,4},{6,5},{7,6},{9,8},{10,9},{11,10},{13,12},{... | collective-permute-start | bytes 24584 | tf_op jit(solution)/shard_map/while/body/eval_jaxpr/ppermute | solution.py:15
  148.8 9.3 %collective-permute-start = (f32[2,8,128]{2,1,0:T(8,128)}, f32[2,8,128]{2,1,0:T(8,128)}, u32[]{:S(2)}, u32[]{:S(2)}) collective-permute-start(f32[2,8,128]{2,1,0:T(8,128)} %get-tuple-element.562), channel_id=1, source_target_pairs={{0,1},{1,2},{2,3},{4,5},{5,6},{6,7},{8,9},{9,10},{10,11},{12,13},{... | collective-permute-start | bytes 24584 | tf_op jit(solution)/shard_map/while/body/eval_jaxpr/ppermute | solution.py:12
  151.6 6.5 %collective-permute-start.1 = (f32[2,8,128]{2,1,0:T(8,128)S(1)}, f32[2,8,128]{2,1,0:T(8,128)}, u32[]{:S(2)}, u32[]{:S(2)}) collective-permute-start(f32[2,8,128]{2,1,0:T(8,128)S(1)} %get-tuple-element.563), channel_id=1, source_target_pairs={{1,0},{2,1},{3,2},{5,4},{6,5},{7,6},{9,8},{10,9},{11,10},{13,12},{... | collective-permute-start | bytes 24584 | tf_op jit(solution)/shard_map/while/body/eval_jaxpr/ppermute | solution.py:15
  163.0 5.9 %collective-permute-start.2 = (f32[2,8,128]{2,1,0:T(8,128)S(1)}, f32[2,8,128]{2,1,0:T(8,128)S(1)}, u32[]{:S(2)}, u32[]{:S(2)}) collective-permute-start(f32[2,8,128]{2,1,0:T(8,128)S(1)} %get-tuple-element.570), channel_id=1, source_target_pairs={{0,1},{1,2},{2,3},{4,5},{5,6},{6,7},{8,9},{9,10},{10,11},{12,13},{... | collective-permute-start | bytes 24584 | tf_op jit(solution)/shard_map/while/body/eval_jaxpr/ppermute | solution.py:12
  183.1 9.3 %collective-permute-start = (f32[2,8,128]{2,1,0:T(8,128)}, f32[2,8,128]{2,1,0:T(8,128)}, u32[]{:S(2)}, u32[]{:S(2)}) collective-permute-start(f32[2,8,128]{2,1,0:T(8,128)} %get-tuple-element.562), channel_id=1, source_target_pairs={{0,1},{1,2},{2,3},{4,5},{5,6},{6,7},{8,9},{9,10},{10,11},{12,13},{... | collective-permute-start | bytes 24584 | tf_op jit(solution)/shard_map/while/body/eval_jaxpr/ppermute | solution.py:12
  185.9 6.5 %collective-permute-start.1 = (f32[2,8,128]{2,1,0:T(8,128)S(1)}, f32[2,8,128]{2,1,0:T(8,128)}, u32[]{:S(2)}, u32[]{:S(2)}) collective-permute-start(f32[2,8,128]{2,1,0:T(8,128)S(1)} %get-tuple-element.563), channel_id=1, source_target_pairs={{1,0},{2,1},{3,2},{5,4},{6,5},{7,6},{9,8},{10,9},{11,10},{13,12},{... | collective-permute-start | bytes 24584 | tf_op jit(solution)/shard_map/while/body/eval_jaxpr/ppermute | solution.py:15
  217.5 9.3 %collective-permute-start = (f32[2,8,128]{2,1,0:T(8,128)}, f32[2,8,128]{2,1,0:T(8,128)}, u32[]{:S(2)}, u32[]{:S(2)}) collective-permute-start(f32[2,8,128]{2,1,0:T(8,128)} %get-tuple-element.562), channel_id=1, source_target_pairs={{0,1},{1,2},{2,3},{4,5},{5,6},{6,7},{8,9},{9,10},{10,11},{12,13},{... | collective-permute-start | bytes 24584 | tf_op jit(solution)/shard_map/while/body/eval_jaxpr/ppermute | solution.py:12
  220.3 6.5 %collective-permute-start.1 = (f32[2,8,128]{2,1,0:T(8,128)S(1)}, f32[2,8,128]{2,1,0:T(8,128)}, u32[]{:S(2)}, u32[]{:S(2)}) collective-permute-start(f32[2,8,128]{2,1,0:T(8,128)S(1)} %get-tuple-element.563), channel_id=1, source_target_pairs={{1,0},{2,1},{3,2},{5,4},{6,5},{7,6},{9,8},{10,9},{11,10},{13,12},{... | collective-permute-start | bytes 24584 | tf_op jit(solution)/shard_map/while/body/eval_jaxpr/ppermute | solution.py:15
  231.6 5.9 %collective-permute-start.2 = (f32[2,8,128]{2,1,0:T(8,128)S(1)}, f32[2,8,128]{2,1,0:T(8,128)S(1)}, u32[]{:S(2)}, u32[]{:S(2)}) collective-permute-start(f32[2,8,128]{2,1,0:T(8,128)S(1)} %get-tuple-element.570), channel_id=1, source_target_pairs={{0,1},{1,2},{2,3},{4,5},{5,6},{6,7},{8,9},{9,10},{10,11},{12,13},{... | collective-permute-start | bytes 24584 | tf_op jit(solution)/shard_map/while/body/eval_jaxpr/ppermute | solution.py:12
  251.8 9.3 %collective-permute-start = (f32[2,8,128]{2,1,0:T(8,128)}, f32[2,8,128]{2,1,0:T(8,128)}, u32[]{:S(2)}, u32[]{:S(2)}) collective-permute-start(f32[2,8,128]{2,1,0:T(8,128)} %get-tuple-element.562), channel_id=1, source_target_pairs={{0,1},{1,2},{2,3},{4,5},{5,6},{6,7},{8,9},{9,10},{10,11},{12,13},{... | collective-permute-start | bytes 24584 | tf_op jit(solution)/shard_map/while/body/eval_jaxpr/ppermute | solution.py:12
  254.6 6.5 %collective-permute-start.1 = (f32[2,8,128]{2,1,0:T(8,128)S(1)}, f32[2,8,128]{2,1,0:T(8,128)}, u32[]{:S(2)}, u32[]{:S(2)}) collective-permute-start(f32[2,8,128]{2,1,0:T(8,128)S(1)} %get-tuple-element.563), channel_id=1, source_target_pairs={{1,0},{2,1},{3,2},{5,4},{6,5},{7,6},{9,8},{10,9},{11,10},{13,12},{... | collective-permute-start | bytes 24584 | tf_op jit(solution)/shard_map/while/body/eval_jaxpr/ppermute | solution.py:15
  287.8 6.8 %collective-permute-start.5 = (f32[2,8,128]{2,1,0:T(8,128)S(1)}, f32[2,8,128]{2,1,0:T(8,128)S(1)}, u32[]{:S(2)}, u32[]{:S(2)}) collective-permute-start(f32[2,8,128]{2,1,0:T(8,128)S(1)} %get-tuple-element.591), channel_id=1, source_target_pairs={{0,1},{1,2},{2,3},{4,5},{5,6},{6,7},{8,9},{9,10},{10,11},{12,13},{... | collective-permute-start | bytes 24584 | tf_op jit(solution)/shard_map/while/body/eval_jaxpr/ppermute | solution.py:12
  321.2 6.5 %collective-permute-start.5 = (f32[2,8,128]{2,1,0:T(8,128)S(1)}, f32[2,8,128]{2,1,0:T(8,128)S(1)}, u32[]{:S(2)}, u32[]{:S(2)}) collective-permute-start(f32[2,8,128]{2,1,0:T(8,128)S(1)} %get-tuple-element.591), channel_id=1, source_target_pairs={{0,1},{1,2},{2,3},{4,5},{5,6},{6,7},{8,9},{9,10},{10,11},{12,13},{... | collective-permute-start | bytes 24584 | tf_op jit(solution)/shard_map/while/body/eval_jaxpr/ppermute | solution.py:12
  347.5 6.5 %collective-permute-start.9 = (f32[2,8,1024]{2,1,0:T(8,128)S(1)}, f32[2,8,1024]{2,1,0:T(8,128)}, u32[]{:S(2)}, u32[]{:S(2)}) collective-permute-start(f32[2,8,1024]{2,1,0:T(8,128)S(1)} %maximum_add_fusion.20), channel_id=1, source_target_pairs={{4,0},{8,4},{12,8},{16,12},{20,16},{24,20},{28,24},{5,1},{9,5},{13... | collective-permute-start | bytes 196616 | tf_op jit(solution)/shard_map/while/body/eval_jaxpr/ppermute | solution.py:23
  355.5 6.4 %collective-permute-start.5 = (f32[2,8,128]{2,1,0:T(8,128)S(1)}, f32[2,8,128]{2,1,0:T(8,128)S(1)}, u32[]{:S(2)}, u32[]{:S(2)}) collective-permute-start(f32[2,8,128]{2,1,0:T(8,128)S(1)} %get-tuple-element.591), channel_id=1, source_target_pairs={{0,1},{1,2},{2,3},{4,5},{5,6},{6,7},{8,9},{9,10},{10,11},{12,13},{... | collective-permute-start | bytes 24584 | tf_op jit(solution)/shard_map/while/body/eval_jaxpr/ppermute | solution.py:12
  381.7 6.0 %collective-permute-start.9 = (f32[2,8,1024]{2,1,0:T(8,128)S(1)}, f32[2,8,1024]{2,1,0:T(8,128)}, u32[]{:S(2)}, u32[]{:S(2)}) collective-permute-start(f32[2,8,1024]{2,1,0:T(8,128)S(1)} %maximum_add_fusion.20), channel_id=1, source_target_pairs={{4,0},{8,4},{12,8},{16,12},{20,16},{24,20},{28,24},{5,1},{9,5},{13... | collective-permute-start | bytes 196616 | tf_op jit(solution)/shard_map/while/body/eval_jaxpr/ppermute | solution.py:23
  389.3 6.4 %collective-permute-start.5 = (f32[2,8,128]{2,1,0:T(8,128)S(1)}, f32[2,8,128]{2,1,0:T(8,128)S(1)}, u32[]{:S(2)}, u32[]{:S(2)}) collective-permute-start(f32[2,8,128]{2,1,0:T(8,128)S(1)} %get-tuple-element.591), channel_id=1, source_target_pairs={{0,1},{1,2},{2,3},{4,5},{5,6},{6,7},{8,9},{9,10},{10,11},{12,13},{... | collective-permute-start | bytes 24584 | tf_op jit(solution)/shard_map/while/body/eval_jaxpr/ppermute | solution.py:12
  415.5 7.2 %collective-permute-start.9 = (f32[2,8,1024]{2,1,0:T(8,128)S(1)}, f32[2,8,1024]{2,1,0:T(8,128)}, u32[]{:S(2)}, u32[]{:S(2)}) collective-permute-start(f32[2,8,1024]{2,1,0:T(8,128)S(1)} %maximum_add_fusion.20), channel_id=1, source_target_pairs={{4,0},{8,4},{12,8},{16,12},{20,16},{24,20},{28,24},{5,1},{9,5},{13... | collective-permute-start | bytes 196616 | tf_op jit(solution)/shard_map/while/body/eval_jaxpr/ppermute | solution.py:23
  424.2 6.4 %collective-permute-start.5 = (f32[2,8,128]{2,1,0:T(8,128)S(1)}, f32[2,8,128]{2,1,0:T(8,128)S(1)}, u32[]{:S(2)}, u32[]{:S(2)}) collective-permute-start(f32[2,8,128]{2,1,0:T(8,128)S(1)} %get-tuple-element.591), channel_id=1, source_target_pairs={{0,1},{1,2},{2,3},{4,5},{5,6},{6,7},{8,9},{9,10},{10,11},{12,13},{... | collective-permute-start | bytes 24584 | tf_op jit(solution)/shard_map/while/body/eval_jaxpr/ppermute | solution.py:12
  456.6 6.4 %collective-permute-start.5 = (f32[2,8,128]{2,1,0:T(8,128)S(1)}, f32[2,8,128]{2,1,0:T(8,128)S(1)}, u32[]{:S(2)}, u32[]{:S(2)}) collective-permute-start(f32[2,8,128]{2,1,0:T(8,128)S(1)} %get-tuple-element.591), channel_id=1, source_target_pairs={{0,1},{1,2},{2,3},{4,5},{5,6},{6,7},{8,9},{9,10},{10,11},{12,13},{... | collective-permute-start | bytes 24584 | tf_op jit(solution)/shard_map/while/body/eval_jaxpr/ppermute | solution.py:12
  489.0 6.4 %collective-permute-start.5 = (f32[2,8,128]{2,1,0:T(8,128)S(1)}, f32[2,8,128]{2,1,0:T(8,128)S(1)}, u32[]{:S(2)}, u32[]{:S(2)}) collective-permute-start(f32[2,8,128]{2,1,0:T(8,128)S(1)} %get-tuple-element.591), channel_id=1, source_target_pairs={{0,1},{1,2},{2,3},{4,5},{5,6},{6,7},{8,9},{9,10},{10,11},{12,13},{... | collective-permute-start | bytes 24584 | tf_op jit(solution)/shard_map/while/body/eval_jaxpr/ppermute | solution.py:12
  521.4 6.4 %collective-permute-start.5 = (f32[2,8,128]{2,1,0:T(8,128)S(1)}, f32[2,8,128]{2,1,0:T(8,128)S(1)}, u32[]{:S(2)}, u32[]{:S(2)}) collective-permute-start(f32[2,8,128]{2,1,0:T(8,128)S(1)} %get-tuple-element.591), channel_id=1, source_target_pairs={{0,1},{1,2},{2,3},{4,5},{5,6},{6,7},{8,9},{9,10},{10,11},{12,13},{... | collective-permute-start | bytes 24584 | tf_op jit(solution)/shard_map/while/body/eval_jaxpr/ppermute | solution.py:12
  (83 other events, 459.1 us)
where the time goes:
time: 563 us; the launch traced here: 553 us
  starting transfers between devices  194 us (34%)
  matrix products  128 us (23%)
  waiting for transfers between devices  115 us (20%)
  local copies, waits for them, and re-layouts  88.1 us (16%)
  other arithmetic  23.1 us (4%)
    ppermute x32, starting transfers between devices, extended(): lax.ppermute(lax.slice_in_dim(block, block.shape[dim] - width, None, axis...  112 us
    ppermute x32, waiting for transfers between devices, extended(): lax.ppermute(lax.slice_in_dim(block, 0, width, axis=dim), axis, backward)  75.9 us
    ppermute x32, starting transfers between devices, extended(): lax.ppermute(lax.slice_in_dim(block, 0, width, axis=dim), axis, backward)  41.2 us
    ppermute x16, starting transfers between devices, from_behind(): lax.ppermute(value, axis, [(source, source + steps) for source in range(l...  41 us
    ppermute x16, waiting for transfers between devices, from_behind(): lax.ppermute(value, axis, [(source, source + steps) for source in range(l...  38.9 us
    dot_general x32, matrix products, block_product(): jnp.einsum(form, shifted[1], blocks[:, :, 0], precision=high)  32.2 us
    dot_general x32, matrix products, block_product(): jnp.einsum(form, shifted[0], blocks[:, :, 0], precision=high)  32.1 us
    dot_general x32, matrix products, block_product(): jnp.einsum(form, shifted[0], blocks[:, :, 1], precision=high)  31.9 us
  transfers between devices with their start and end apart: 80, of which 40 were waited for; matrix products, arithmetic and copies ran while one was open for 12% of the time, Pallas kernels for 0%

commit v1 on v0

v1 whole, which is shorter than its diff:
```python
import functools
import jax
import jax.numpy as jnp
from jax import lax
from jax.experimental import pallas as pl
from jax.experimental.pallas import tpu as pltpu
from jax.sharding import PartitionSpec as P

F32 = jnp.float32
BF16 = jnp.bfloat16
MESH = pl.DeviceIdType.MESH
DOWN, UP = 0, 1
CENTRE, LEFT, RIGHT = 0, 1, 2


def split(value):
    high = value.astype(BF16)
    low = (value - high.astype(F32)).astype(BF16)
    return high, low


def kernel(
    depth_count, lat_count, cell_ref, layer_ref, rhs_ref, couple_ref, factor_ref,
    waves_ref, field_ref,
    raw, weights, edge_raw, edge_weights, rhs_halo, couple_halo,
    forcing0, forcing1, coef, source, inner, main_in, left_in, right_in,
    extra_left, extra_right, out_ext,
    load_sem, halo_send, halo_recv, edge_send, edge_recv, hop_send, hop_recv,
):
    tiles = factor_ref.shape[1]
    tile = factor_ref.shape[-1]
    cells = rhs_ref.shape[-1]
    shots = rhs_ref.shape[2]
    wide = cells + 2 * tile
    d = lax.axis_index("depth")
    l = lax.axis_index("lat")
    has_left, has_right = l > 0, l < lat_count - 1
    has_above, has_below = d > 0, d < depth_count - 1

    def load(layer, t):
        return pltpu.make_async_copy(factor_ref.at[layer, t], raw.at[layer, t], load_sem.at[layer, t])

    for layer in range(2):
        for t in range(tiles):
            load(layer, t).start()

    main_in[...] = jnp.zeros_like(main_in)
    left_in[...] = jnp.zeros_like(left_in)
    right_in[...] = jnp.zeros_like(right_in)
    extra_left[...] = jnp.zeros_like(extra_left)
    extra_right[...] = jnp.zeros_like(extra_right)
    rhs_halo[...] = jnp.zeros_like(rhs_halo)
    couple_halo[...] = jnp.zeros_like(couple_halo)

    @pl.when(l == 0)
    def _():
        edge_raw[:, 0] = jnp.zeros_like(edge_raw[:, 0])

    @pl.when(l == lat_count - 1)
    def _():
        edge_raw[:, 1] = jnp.zeros_like(edge_raw[:, 1])

    barrier = pltpu.get_barrier_semaphore()
    steps = [(a, b) for a in (-1, 0, 1) for b in (-1, 0, 1) if (a, b) != (0, 0)]

    def reachable(a, b):
        return (d + a >= 0) & (d + a < depth_count) & (l + b >= 0) & (l + b < lat_count)

    for a, b in steps:
        @pl.when(reachable(a, b))
        def _():
            pl.semaphore_signal(barrier, inc=1, device_id=(d + a, l + b), device_id_type=MESH)
    rows = 1 + has_above.astype(jnp.int32) + has_below.astype(jnp.int32)
    columns = 1 + has_left.astype(jnp.int32) + has_right.astype(jnp.int32)
    pl.semaphore_wait(barrier, rows * columns - 1)

    def rhs_copy(side):
        cut = pl.ds(cells - tile, tile) if side == 0 else pl.ds(0, tile)
        to = (d, l + 1) if side == 0 else (d, l - 1)
        return pltpu.make_async_remote_copy(
            src_ref=rhs_ref.at[:, 0, :, cut], dst_ref=rhs_halo.at[side],
            send_sem=halo_send.at[0, side], recv_sem=halo_recv.at[0, side],
            device_id=to, device_id_type=MESH)

    def couple_copy(side):
        cut = pl.ds(cells - tile, tile) if side == 0 else pl.ds(0, tile)
        to = (d, l + 1) if side == 0 else (d, l - 1)
        return pltpu.make_async_remote_copy(
            src_ref=couple_ref.at[:, :, :, cut], dst_ref=couple_halo.at[side],
            send_sem=halo_send.at[1, side], recv_sem=halo_recv.at[1, side],
            device_id=to, device_id_type=MESH)

    def edge_copy(layer, side):
        t, j = (tiles - 1, 2) if side == 0 else (0, 0)
        to = (d, l + 1) if side == 0 else (d, l - 1)
        return pltpu.make_async_remote_copy(
            src_ref=factor_ref.at[layer, t, j], dst_ref=edge_raw.at[layer, side],
            send_sem=edge_send.at[layer, side], recv_sem=edge_recv.at[layer, side],
            device_id=to, device_id_type=MESH)

    def sends(side):
        return has_right if side == 0 else has_left

    def receives(side):
        return has_left if side == 0 else has_right

    def hop_copies(way):
        step = 1 if way == DOWN else -1
        onward = has_below if way == DOWN else has_above
        behind = has_above if way == DOWN else has_below
        made = []
        for num, (src, dst, to, go, come) in enumerate((
            (out_ext.at[way, :, :, pl.ds(cells, 2 * tile)], left_in.at[way], (d + step, l + 1),
             onward & has_right, behind & has_left),
            (out_ext.at[way, :, :, pl.ds(0, 2 * tile)], right_in.at[way], (d + step, l - 1),
             onward & has_left, behind & has_right),
            (out_ext.at[way], main_in.at[way], (d + step, l), onward, behind),
            (out_ext.at[way, :, :, pl.ds(cells + tile, tile)], extra_left.at[way], (d, l + 1),
             has_right, has_left),
            (out_ext.at[way, :, :, pl.ds(0, tile)], extra_right.at[way], (d, l - 1),
             has_left, has_right),
        )):
            made.append((pltpu.make_async_remote_copy(
                src_ref=src, dst_ref=dst, send_sem=hop_send.at[way, num], recv_sem=hop_recv.at[way, num],
                device_id=to, device_id_type=MESH), go, come))
        return made

    for side in range(2):
        @pl.when(sends(side))
        def _():
            rhs_copy(side).start()
            couple_copy(side).start()
    for layer in (1, 0):
        for side in range(2):
            @pl.when(sends(side))
            def _():
                edge_copy(layer, side).start()

    def convert(layer):
        def body(t, carry):
            load(layer, t).wait()
            for j in range(3):
                for c in range(2):
                    high, low = split(raw[layer, t, j, c])
                    weights[layer, t, pl.ds(j * tile, tile), pl.ds(c * tile, tile)] = high
                    weights[layer, t, pl.ds((3 + j) * tile, tile), pl.ds(c * tile, tile)] = low
            return carry
        lax.fori_loop(0, tiles, body, 0)

    def convert_edge(layer):
        for side in range(2):
            @pl.when(receives(side))
            def _():
                edge_copy(layer, side).wait_recv()
            for c in range(2):
                high, low = split(edge_raw[layer, side, c])
                edge_weights[layer, side, pl.ds(0, tile), pl.ds(c * tile, tile)] = high
                edge_weights[layer, side, pl.ds(tile, tile), pl.ds(c * tile, tile)] = low

    convert(0)
    convert(1)

    row = lax.broadcasted_iota(jnp.int32, (shots, tile), 0)
    lane = lax.broadcasted_iota(jnp.int32, (shots, tile), 1)
    src_cell = jnp.zeros((shots, tile), jnp.int32)
    src_layer = jnp.zeros((shots, tile), jnp.int32)
    for s in range(shots):
        src_cell = jnp.where(row == s, cell_ref[s], src_cell)
        src_layer = jnp.where(row == s, layer_ref[s], src_layer)

    def pulse(layer, block):
        hit = (src_layer == d * 2 + layer) & (src_cell == l * cells + block * tile + lane)
        return jnp.where(hit, 4.0, 0.0).astype(F32)

    for side in range(2):
        @pl.when(receives(side))
        def _():
            rhs_copy(side).wait_recv()
            couple_copy(side).wait_recv()
        block = -1 if side == 0 else tiles
        at = pl.ds((block + 1) * tile, tile)
        forcing0[0, :, at] = rhs_halo[side, 0] + pulse(0, block)
        forcing0[1, :, at] = rhs_halo[side, 1]
        for c in range(2):
            coef[DOWN, c, :, at] = jnp.broadcast_to(couple_halo[side, DOWN, c, 0:1, :], (shots, tile))
            coef[UP, c, :, at] = jnp.broadcast_to(couple_halo[side, UP, c, 1:2, :], (shots, tile))
    for block in range(tiles):
        at = pl.ds(block * tile, tile)
        to = pl.ds((block + 1) * tile, tile)
        forcing0[0, :, to] = rhs_ref[0, 0, :, at] + pulse(0, block)
        forcing0[1, :, to] = rhs_ref[1, 0, :, at]
        forcing1[0, :, at] = rhs_ref[0, 1, :, at] + pulse(1, block)
        forcing1[1, :, at] = rhs_ref[1, 1, :, at]
        for c in range(2):
            coef[DOWN, c, :, to] = jnp.broadcast_to(couple_ref[DOWN, c, 0:1, at], (shots, tile))
            coef[UP, c, :, to] = jnp.broadcast_to(couple_ref[UP, c, 1:2, at], (shots, tile))
    convert_edge(1)

    def put(target, at, real_part, imag_part):
        for c, value in enumerate((real_part, imag_part)):
            high, low = split(value)
            target[pl.ds(c * shots, shots), at] = high
            target[pl.ds((2 + c) * shots, shots), at] = low

    def product(left_side, right_side):
        both = jnp.dot(left_side, right_side, preferred_element_type=F32)
        both = both[: 2 * shots] + both[2 * shots:]
        real_part = both[:shots, :tile] - both[shots:, tile:]
        imag_part = both[:shots, tile:] + both[shots:, :tile]
        return real_part, imag_part

    def row_block(from_ref, layer, t):
        value = from_ref[:, pl.ds(t * tile, 3 * tile)]
        return product(jnp.concatenate([value, value], axis=1), weights[layer, t])

    def edge_block(from_ref, layer, side):
        block = 0 if side == 0 else tiles - 1
        value = from_ref[:, pl.ds((block + 1) * tile, tile)]
        return product(jnp.concatenate([value, value], axis=1), edge_weights[layer, side])

    def arrived(way, block):
        at = pl.ds((block + 1) * tile, tile)
        parts = []
        for c in range(2):
            value = main_in[way, c, :, at]
            if block <= 0:
                value = value + left_in[way, c, :, pl.ds((block + 1) * tile, tile)]
            if block >= tiles - 1:
                value = value + right_in[way, c, :, pl.ds((block - tiles + 1) * tile, tile)]
            parts.append(value)
        return parts

    zero16 = jnp.zeros((4 * shots, tile), BF16)
    inner[:, pl.ds(0, tile)] = zero16
    inner[:, pl.ds(cells + tile, tile)] = zero16

    def column_step(way, layer, base):
        for side in range(2):
            block = -1 if side == 0 else tiles
            at = pl.ds((block + 1) * tile, tile)
            real_part, imag_part = edge_block(inner, layer, side)
            out_ext[way, 0, :, at] = real_part
            out_ext[way, 1, :, at] = imag_part
        copies = hop_copies(way)
        order = [0, tiles - 1] + list(range(1, tiles - 1))
        for t in order:
            real_part, imag_part = row_block(inner, layer, t)
            if base is not None:
                real_part = real_part + base[0, layer, :, pl.ds(t * tile, tile)]
                imag_part = imag_part + base[1, layer, :, pl.ds(t * tile, tile)]
            at = pl.ds((t + 1) * tile, tile)
            out_ext[way, 0, :, at] = real_part
            out_ext[way, 1, :, at] = imag_part
            if t == tiles - 1:
                for copy, go, _ in copies[:2]:
                    pl.when(go)(copy.start)
        for copy, go, _ in copies[2:]:
            pl.when(go)(copy.start)

    def await_hop(way, first, last):
        for copy, _, come in hop_copies(way)[first:last]:
            pl.when(come)(copy.wait_recv)

    def total(way, result, layer):
        await_hop(way, 3, 5)
        for c in range(2):
            result[c, layer] = out_ext[way, c, :, pl.ds(tile, cells)]
            low, high = pl.ds(0, tile), pl.ds(cells - tile, tile)
            result[c, layer, :, low] = out_ext[way, c, :, pl.ds(tile, tile)] + extra_left[way, c]
            result[c, layer, :, high] = out_ext[way, c, :, pl.ds(cells, tile)] + extra_right[way, c]

    await_hop(DOWN, 0, 3)
    for block in range(-1, tiles + 1):
        at = pl.ds((block + 1) * tile, tile)
        real_in, imag_in = arrived(DOWN, block)
        real_coef, imag_coef = coef[DOWN, 0, :, at], coef[DOWN, 1, :, at]
        put(source, at,
            forcing0[0, :, at] + real_coef * real_in - imag_coef * imag_in,
            forcing0[1, :, at] + real_coef * imag_in + imag_coef * real_in)
    for t in range(tiles):
        at = pl.ds(t * tile, tile)
        real_part, imag_part = row_block(source, 0, t)
        waves_ref[0, 0, :, at] = real_part
        waves_ref[1, 0, :, at] = imag_part
        real_coef, imag_coef = couple_ref[DOWN, 0, 1:2, at], couple_ref[DOWN, 1, 1:2, at]
        put(inner, pl.ds((t + 1) * tile, tile),
            forcing1[0, :, at] + real_coef * real_part - imag_coef * imag_part,
            forcing1[1, :, at] + real_coef * imag_part + imag_coef * real_part)
    column_step(DOWN, 1, None)
    convert_edge(0)
    total(DOWN, waves_ref, 1)

    @pl.when(d == depth_count - 1)
    def _():
        field_ref[:, 1] = waves_ref[:, 1]

    @pl.when(has_below)
    def _():
        await_hop(UP, 0, 3)
        for block in range(-1, tiles + 1):
            at = pl.ds((block + 1) * tile, tile)
            real_in, imag_in = arrived(UP, block)
            real_coef, imag_coef = coef[UP, 0, :, at], coef[UP, 1, :, at]
            put(source, at,
                real_coef * real_in - imag_coef * imag_in,
                real_coef * imag_in + imag_coef * real_in)
        for t in range(tiles):
            at = pl.ds(t * tile, tile)
            real_part, imag_part = row_block(source, 1, t)
            field_ref[0, 1, :, at] = waves_ref[0, 1, :, at] + real_part
            field_ref[1, 1, :, at] = waves_ref[1, 1, :, at] + imag_part

    for t in range(tiles):
        at = pl.ds(t * tile, tile)
        real_part, imag_part = field_ref[0, 1, :, at], field_ref[1, 1, :, at]
        real_coef, imag_coef = couple_ref[UP, 0, 0:1, at], couple_ref[UP, 1, 0:1, at]
        put(inner, pl.ds((t + 1) * tile, tile),
            real_coef * real_part - imag_coef * imag_part,
            real_coef * imag_part + imag_coef * real_part)
    column_step(UP, 0, waves_ref)
    total(UP, field_ref, 0)

    for side in range(2):
        @pl.when(sends(side))
        def _():
            rhs_copy(side).wait_send()
            couple_copy(side).wait_send()
            edge_copy(0, side).wait_send()
            edge_copy(1, side).wait_send()
    for way in (DOWN, UP):
        for copy, go, _ in hop_copies(way):
            pl.when(go)(copy.wait_send)


def shards(depth_count, lat_count, rhs_field, src_cell, src_layer, factor, couple):
    layers, tiles = factor.shape[:2]
    tile = factor.shape[-1]
    shots, cells = rhs_field.shape[2:]
    assert layers == 2 and cells == tiles * tile
    wide = cells + 2 * tile
    vmem, smem = pl.BlockSpec(memory_space=pltpu.VMEM), pl.BlockSpec(memory_space=pltpu.SMEM)
    dma = pltpu.SemaphoreType.DMA
    return pl.pallas_call(
        functools.partial(kernel, depth_count, lat_count),
        out_shape=[jax.ShapeDtypeStruct(rhs_field.shape, F32)] * 2,
        in_specs=[smem, smem, vmem, vmem, pl.BlockSpec(memory_space=pl.ANY)],
        out_specs=[vmem, vmem],
        scratch_shapes=[
            pltpu.VMEM(factor.shape, F32),
            pltpu.VMEM((2, tiles, 6 * tile, 2 * tile), BF16),
            pltpu.VMEM((2, 2, 2, tile, tile), F32),
            pltpu.VMEM((2, 2, 2 * tile, 2 * tile), BF16),
            pltpu.VMEM((2, 2, shots, tile), F32),
            pltpu.VMEM((2, 2, 2, 2, tile), F32),
            pltpu.VMEM((2, shots, wide), F32),
            pltpu.VMEM((2, shots, cells), F32),
            pltpu.VMEM((2, 2, shots, wide), F32),
            pltpu.VMEM((4 * shots, wide), BF16),
            pltpu.VMEM((4 * shots, wide), BF16),
            pltpu.VMEM((2, 2, shots, wide), F32),
            pltpu.VMEM((2, 2, shots, 2 * tile), F32),
            pltpu.VMEM((2, 2, shots, 2 * tile), F32),
            pltpu.VMEM((2, 2, shots, tile), F32),
            pltpu.VMEM((2, 2, shots, tile), F32),
            pltpu.VMEM((2, 2, shots, wide), F32),
            dma((2, tiles)), dma((2, 2)), dma((2, 2)), dma((2, 2)), dma((2, 2)), dma((2, 5)), dma((2, 5)),
        ],
        compiler_params=pltpu.CompilerParams(
            collective_id=0, has_side_effects=True, vmem_limit_bytes=40 * 1024 * 1024),
        name="sweeps",
    )(src_cell, src_layer, rhs_field, couple, factor)


def solution(mesh):
    placed = (
        P(None, "depth", None, "lat"),
        P(),
        P(),
        P("depth", "lat", None, None, None, None),
        P(None, None, "depth", "lat"),
    )
    return jax.shard_map(
        functools.partial(shards, mesh.shape["depth"], mesh.shape["lat"]),
        mesh=mesh,
        in_specs=placed,
        out_specs=(P(None, "depth", None, "lat"), P(None, "depth", None, "lat")),
        check_vma=False,
    )
```

time: 563 us -> 82.4 us (0.15); the launches traced: 553 us -> 82.1 us
  starting transfers between devices: 194 us -> 0 us
  matrix products: 128 us -> 0 us
  waiting for transfers between devices: 115 us -> 0 us
  local copies, waits for them, and re-layouts: 88.1 us -> 7.06 us
  Pallas kernels: 0 us -> 74.4 us
  other arithmetic: 23.1 us -> 0 us
    ppermute x80 -> x0, starting transfers between devices: 194 us -> none  [the longest x32 112 us: extended(): lax.ppermute(lax.slice_in_dim(block, block.shape[dim] - width, None, axis...]
    dot_general x128 -> x0, matrix products: 128 us -> none  [the longest x32 32.2 us: block_product(): jnp.einsum(form, shifted[1], blocks[:, :, 0], precision=high)]
    ppermute x80 -> x0, waiting for transfers between devices: 115 us -> none  [the longest x32 75.9 us: extended(): lax.ppermute(lax.slice_in_dim(block, 0, width, axis=dim), axis, backward)]
    pallas_call x0 -> x1, Pallas kernels: none -> 74.4 us  [shards(): pl.pallas_call(functools.partial(kernel, depth_count, lat_count), out_sha...]
    squeeze x25 -> x0, local copies, waits for them, and re-layouts: 68.3 us -> none  [the longest x8 26.2 us: ascend(): factor[layer_num]]
    reshape x32 -> x0, other arithmetic: 11.8 us -> none  [block_product(): jnp.stack([padded[:, :, offset * tile_cells:offset * tile_cells + strip_c...]
    slice x32 -> x0, local copies, waits for them, and re-layouts: 11.2 us -> none  [the longest x16 6.42 us: complex_scale(): real_part = coef[0][None, :] * vector[0] - coef[1][None, :] * vector[1]]
    sub x24 -> x0, other arithmetic: 6.52 us -> none  [complex_scale(): real_part = coef[0][None, :] * vector[0] - coef[1][None, :] * vector[1]]
  transfers between devices with their start and end apart: 80 -> 0, of which waited for: 40 -> 0; matrix products, arithmetic and copies ran while one was open for 12% -> 0% of each run, Pallas kernels for 0% -> 0%
where the time goes in v1:
time: 82.4 us; the launch traced here: 82.1 us
  Pallas kernels  74.4 us (90%)
  local copies, waits for them, and re-layouts  7.06 us (9%)
    pallas_call x1, Pallas kernels, shards(): pl.pallas_call(functools.partial(kernel, depth_count, lat_count), out_sha...  74.4 us
    unnamed x12, local copies, waits for them, and re-layouts  7.06 us

profile of v1, /device:TPU:0, one launch (start us, length us, event | category | flops | bytes accessed | tf_op | source)
XLA Modules:
  0.0 82.1 jit_solution(14102646603860493643)
XLA Ops:
  0.6 0.0 copy-start
  0.6 2.8 %copy-done = f32[2,8,3,2,128,128]{5,4,3,2,1,0:T(8,128)S(1)} copy-done((f32[2,8,3,2,128,128]{5,4,3,2,1,0:T(8,128)S(1)}, f32[2,8,3,2,128,128]{5,4,3,2,1,0:T(8,128)}, u32[]{:S(2)}) %copy-start) | copy-done | bytes 6291480
  3.4 0.0 copy-start.1
  3.4 0.9 %copy-done.1 = f32[2,2,8,1024]{3,2,1,0:T(8,128)S(1)} copy-done((f32[2,2,8,1024]{3,2,1,0:T(8,128)S(1)}, f32[2,2,8,1024]{3,2,1,0:T(8,128)}, u32[]{:S(2)}) %copy-start.1) | copy-done | bytes 131096
  4.3 0.0 copy-start.2
  4.3 0.8 copy-done.2
  5.1 0.0 copy-start.3
  5.1 0.7 copy-done.3
  5.7 0.0 copy-start.4
  5.7 0.7 copy-done.4
  6.4 74.4 %sweeps.1 = (f32[2,2,8,1024]{3,2,1,0:T(8,128)S(1)}, f32[2,2,8,1024]{3,2,1,0:T(8,128)S(1)}) custom-call(s32[8]{0:T(128)S(1)} %copy-done.3, s32[8]{0:T(128)S(1)} %copy-done.4, f32[2,2,8,1024]{3,2,1,0:T(8,128)S(1)} %copy-done.1, f32[2,2,2,1024]{3,2,1,0:T(2,128)S(1)} %copy-done.2, f32[2,8,3,2,128,128]{5,4,3,2,1,0:T(8,128)S(1)} %copy-done), custom_call_target="tpu_custom_call" | custom-call | tf_op jit(solution)/shard_map/sweeps/pallas_call | solution.py:343
  80.8 0.7 copy.9
  81.5 0.7 copy.10
Async XLA Ops:
  0.6 2.8 %copy-start = (f32[2,8,3,2,128,128]{5,4,3,2,1,0:T(8,128)S(1)}, f32[2,8,3,2,128,128]{5,4,3,2,1,0:T(8,128)}, u32[]{:S(2)}) copy-start(f32[2,8,3,2,128,128]{5,4,3,2,1,0:T(8,128)} %factor_ref.1) | copy-start | bytes 18874372
  3.4 0.9 %copy-start.1 = (f32[2,2,8,1024]{3,2,1,0:T(8,128)S(1)}, f32[2,2,8,1024]{3,2,1,0:T(8,128)}, u32[]{:S(2)}) copy-start(f32[2,2,8,1024]{3,2,1,0:T(8,128)} %rhs_ref.1) | copy-start | bytes 393220
  4.3 0.8 copy-start.2
  5.1 0.7 copy-start.3
  5.7 0.7 copy-start.4

commit v2 on v1

--- a/solution.py
+++ b/solution.py
@@ -20,17 +20,17 @@
 
 
 def kernel(
-    depth_count, lat_count, cell_ref, layer_ref, rhs_ref, couple_ref, factor_ref,
+    depth_count, lat_count, cell_hbm, layer_hbm, rhs_hbm, couple_hbm, factor_ref,
     waves_ref, field_ref,
-    raw, weights, edge_raw, edge_weights, rhs_halo, couple_halo,
+    cell_ref, layer_ref, rhs_ref, couple_ref, raw, weights, edge_raw, edge_weights, rhs_halo, couple_halo,
     forcing0, forcing1, coef, source, inner, main_in, left_in, right_in,
     extra_left, extra_right, out_ext,
-    load_sem, halo_send, halo_recv, edge_send, edge_recv, hop_send, hop_recv,
+    small_sem, load_sem, halo_send, halo_recv, edge_send, edge_recv, hop_send, hop_recv,
 ):
     tiles = factor_ref.shape[1]
     tile = factor_ref.shape[-1]
-    cells = rhs_ref.shape[-1]
-    shots = rhs_ref.shape[2]
+    cells = rhs_hbm.shape[-1]
+    shots = rhs_hbm.shape[2]
     wide = cells + 2 * tile
     d = lax.axis_index("depth")
     l = lax.axis_index("lat")
@@ -40,6 +40,13 @@
     def load(layer, t):
         return pltpu.make_async_copy(factor_ref.at[layer, t], raw.at[layer, t], load_sem.at[layer, t])
 
+    small = [
+        pltpu.make_async_copy(src, dst, small_sem.at[num])
+        for num, (src, dst) in enumerate((
+            (rhs_hbm, rhs_ref), (couple_hbm, couple_ref), (cell_hbm, cell_ref), (layer_hbm, layer_ref)))
+    ]
+    for copy in small:
+        copy.start()
     for layer in range(2):
         for t in range(tiles):
             load(layer, t).start()
@@ -78,7 +85,7 @@
         cut = pl.ds(cells - tile, tile) if side == 0 else pl.ds(0, tile)
         to = (d, l + 1) if side == 0 else (d, l - 1)
         return pltpu.make_async_remote_copy(
-            src_ref=rhs_ref.at[:, 0, :, cut], dst_ref=rhs_halo.at[side],
+            src_ref=rhs_hbm.at[:, 0, :, cut], dst_ref=rhs_halo.at[side],
             send_sem=halo_send.at[0, side], recv_sem=halo_recv.at[0, side],
             device_id=to, device_id_type=MESH)
 
@@ -86,7 +93,7 @@
         cut = pl.ds(cells - tile, tile) if side == 0 else pl.ds(0, tile)
         to = (d, l + 1) if side == 0 else (d, l - 1)
         return pltpu.make_async_remote_copy(
-            src_ref=couple_ref.at[:, :, :, cut], dst_ref=couple_halo.at[side],
+            src_ref=couple_hbm.at[:, :, :, cut], dst_ref=couple_halo.at[side],
             send_sem=halo_send.at[1, side], recv_sem=halo_recv.at[1, side],
             device_id=to, device_id_type=MESH)
 
@@ -109,12 +116,17 @@
         onward = has_below if way == DOWN else has_above
         behind = has_above if way == DOWN else has_below
         made = []
+        blocks = tiles + 2
+        middle = blocks // 2
+        chunks = [(0, 2), (blocks - 2, blocks), (2, middle), (middle, blocks - 2)]
         for num, (src, dst, to, go, come) in enumerate((
+            (out_ext.at[way, :, :, pl.ds(0, 2 * tile)], right_in.at[way], (d + step, l - 1),
+             onward & has_left, behind & has_right),
             (out_ext.at[way, :, :, pl.ds(cells, 2 * tile)], left_in.at[way], (d + step, l + 1),
              onward & has_right, behind & has_left),
-            (out_ext.at[way, :, :, pl.ds(0, 2 * tile)], right_in.at[way], (d + step, l - 1),
-             onward & has_left, behind & has_right),
-            (out_ext.at[way], main_in.at[way], (d + step, l), onward, behind),
+            *((out_ext.at[way, :, :, pl.ds(first * tile, (last - first) * tile)],
+               main_in.at[way, :, :, pl.ds(first * tile, (last - first) * tile)],
+               (d + step, l), onward, behind) for first, last in chunks),
             (out_ext.at[way, :, :, pl.ds(cells + tile, tile)], extra_left.at[way], (d, l + 1),
              has_right, has_left),
             (out_ext.at[way, :, :, pl.ds(0, tile)], extra_right.at[way], (d, l - 1),
@@ -159,6 +171,9 @@
 
     convert(0)
     convert(1)
+
+    for copy in small:
+        copy.wait()
 
     row = lax.broadcasted_iota(jnp.int32, (shots, tile), 0)
     lane = lax.broadcasted_iota(jnp.int32, (shots, tile), 1)
@@ -251,25 +266,24 @@
             at = pl.ds((t + 1) * tile, tile)
             out_ext[way, 0, :, at] = real_part
             out_ext[way, 1, :, at] = imag_part
-            if t == tiles - 1:
-                for copy, go, _ in copies[:2]:
-                    pl.when(go)(copy.start)
-        for copy, go, _ in copies[2:]:
-            pl.when(go)(copy.start)
+            starts = {0: (0, 2), tiles - 1: (1, 3), tiles // 2 - 1: (4,), tiles - 2: (5, 6, 7)}
+            for num in starts.get(t, ()):
+                copy, go, _ = copies[num]
+                pl.when(go)(copy.start)
 
     def await_hop(way, first, last):
         for copy, _, come in hop_copies(way)[first:last]:
             pl.when(come)(copy.wait_recv)
 
     def total(way, result, layer):
-        await_hop(way, 3, 5)
+        await_hop(way, 6, 8)
         for c in range(2):
             result[c, layer] = out_ext[way, c, :, pl.ds(tile, cells)]
             low, high = pl.ds(0, tile), pl.ds(cells - tile, tile)
             result[c, layer, :, low] = out_ext[way, c, :, pl.ds(tile, tile)] + extra_left[way, c]
             result[c, layer, :, high] = out_ext[way, c, :, pl.ds(cells, tile)] + extra_right[way, c]
 
-    await_hop(DOWN, 0, 3)
+    await_hop(DOWN, 0, 6)
     for block in range(-1, tiles + 1):
         at = pl.ds((block + 1) * tile, tile)
         real_in, imag_in = arrived(DOWN, block)
@@ -296,7 +310,7 @@
 
     @pl.when(has_below)
     def _():
-        await_hop(UP, 0, 3)
+        await_hop(UP, 0, 6)
         for block in range(-1, tiles + 1):
             at = pl.ds((block + 1) * tile, tile)
             real_in, imag_in = arrived(UP, block)
@@ -338,14 +352,18 @@
     shots, cells = rhs_field.shape[2:]
     assert layers == 2 and cells == tiles * tile
     wide = cells + 2 * tile
-    vmem, smem = pl.BlockSpec(memory_space=pltpu.VMEM), pl.BlockSpec(memory_space=pltpu.SMEM)
+    vmem = pl.BlockSpec(memory_space=pltpu.VMEM)
     dma = pltpu.SemaphoreType.DMA
     return pl.pallas_call(
         functools.partial(kernel, depth_count, lat_count),
         out_shape=[jax.ShapeDtypeStruct(rhs_field.shape, F32)] * 2,
-        in_specs=[smem, smem, vmem, vmem, pl.BlockSpec(memory_space=pl.ANY)],
+        in_specs=[pl.BlockSpec(memory_space=pltpu.HBM)] * 5,
         out_specs=[vmem, vmem],
         scratch_shapes=[
+            pltpu.SMEM(src_cell.shape, jnp.int32),
+            pltpu.SMEM(src_layer.shape, jnp.int32),
+            pltpu.VMEM(rhs_field.shape, F32),
+            pltpu.VMEM(couple.shape, F32),
             pltpu.VMEM(factor.shape, F32),
             pltpu.VMEM((2, tiles, 6 * tile, 2 * tile), BF16),
             pltpu.VMEM((2, 2, 2, tile, tile), F32),
@@ -363,10 +381,10 @@
             pltpu.VMEM((2, 2, shots, tile), F32),
             pltpu.VMEM((2, 2, shots, tile), F32),
             pltpu.VMEM((2, 2, shots, wide), F32),
-            dma((2, tiles)), dma((2, 2)), dma((2, 2)), dma((2, 2)), dma((2, 2)), dma((2, 5)), dma((2, 5)),
+            dma((4,)), dma((2, tiles)), dma((2, 2)), dma((2, 2)), dma((2, 2)), dma((2, 2)), dma((2, 8)), dma((2, 8)),
         ],
         compiler_params=pltpu.CompilerParams(
-            collective_id=0, has_side_effects=True, vmem_limit_bytes=40 * 1024 * 1024),
+            collective_id=0, has_side_effects=True, vmem_limit_bytes=63 * 1024 * 1024),
         name="sweeps",
     )(src_cell, src_layer, rhs_field, couple, factor)
 

time: 82.4 us -> 75.3 us (0.914)
  local copies, waits for them, and re-layouts: 7.06 us -> 3.14 us
  Pallas kernels: 74.4 us -> 71.4 us
    unnamed x12 -> x2, local copies, waits for them, and re-layouts: 7.06 us -> 3.14 us
    pallas_call x1, Pallas kernels: 74.4 us -> 71.4 us  [shards(): pl.pallas_call(functools.partial(kernel, depth_count, lat_count), out_sha...]
where the time goes in v2:
time: 75.3 us; the launch traced here: 75.1 us
  Pallas kernels  71.4 us (95%)
  local copies, waits for them, and re-layouts  3.14 us (4%)
    pallas_call x1, Pallas kernels, shards(): pl.pallas_call(functools.partial(kernel, depth_count, lat_count), out_sha...  71.4 us
    unnamed x2, local copies, waits for them, and re-layouts  3.14 us

profile of v2, /device:TPU:0, one launch (start us, length us, event | category | flops | bytes accessed | tf_op | source)
XLA Modules:
  0.0 75.1 jit_solution(2720770535766059064)
XLA Ops:
  0.6 71.4 %sweeps.1 = (f32[2,2,8,1024]{3,2,1,0:T(8,128)}, f32[2,2,8,1024]{3,2,1,0:T(8,128)}) custom-call(s32[8]{0:T(128)} %cell_hbm.1, s32[8]{0:T(128)} %layer_hbm.1, f32[2,2,8,1024]{3,2,1,0:T(8,128)} %rhs_hbm.1, f32[2,2,2,1024]{3,2,1,0:T(2,128)} %couple_hbm.1, f32[2,8,3,2,128,128]{5,4,3,2,1,0:T(8,128)} %factor_ref.1), custom_call_target="tpu_custom_call" | custom-call | tf_op jit(solution)/shard_map/sweeps/pallas_call | solution.py:357
  72.0 1.6 %copy.9 = f32[2,2,8,1024]{3,2,1,0:T(8,128)} copy(f32[2,2,8,1024]{3,2,1,0:T(8,128)} %get-tuple-element.4) | data formatting | bytes 262144
  73.6 1.6 %copy.10 = f32[2,2,8,1024]{3,2,1,0:T(8,128)} copy(f32[2,2,8,1024]{3,2,1,0:T(8,128)} %get-tuple-element.5) | data formatting | bytes 262144

commit v3 on v0

v3 whole, which is shorter than its diff:
```python
import functools
import jax
import jax.numpy as jnp
from jax import lax
from jax.experimental import pallas as pl
from jax.experimental.pallas import tpu as pltpu
from jax.sharding import PartitionSpec as P

F32 = jnp.float32
BF16 = jnp.bfloat16
MESH = pl.DeviceIdType.MESH
DOWN, UP = 0, 1
CENTRE, LEFT, RIGHT = 0, 1, 2


def split(value):
    high = value.astype(BF16)
    low = (value - high.astype(F32)).astype(BF16)
    return high, low


def kernel(
    depth_count, lat_count, cell_hbm, layer_hbm, rhs_hbm, couple_hbm, factor_ref,
    waves_ref, field_ref,
    cell_ref, layer_ref, rhs, couple, raw, weights, edge_raw, edge_weights,
    source, inner, out_ext, main_in, left_in, right_in, side_left, side_right,
    extra_left, extra_right, waves, field, result_in,
    small_sem, self_sem, load_sem, part_send, part_recv, mid_send, mid_recv, mid_self,
    edge_send, edge_recv, strip_send, strip_recv, halo_send, halo_recv,
    hop_send, hop_recv, side_send, side_recv, result_send, result_recv,
):
    tile = factor_ref.shape[-1]
    tiles = factor_ref.shape[1] // 2
    cells = tiles * tile
    shots = rhs_hbm.shape[2]
    wide = cells + 2 * tile
    d = lax.axis_index("depth")
    l = lax.axis_index("lat")
    core = lax.rem(d, 2)
    other = 1 - core
    pair = lax.div(d, 2)
    half = 2 * l + core
    pairs, halves = depth_count // 2, 2 * lat_count
    has_left, has_right = half > 0, half < halves - 1
    has_above, has_below = pair > 0, pair < pairs - 1
    partner = (2 * pair + other, l)

    def place(pair_step, half_step):
        spot = half + half_step
        return (2 * (pair + pair_step) + lax.rem(spot + 2, 2), lax.div(spot + 2, 2) - 1)

    def remote(src, dst, send_sem, recv_sem, to):
        return pltpu.make_async_remote_copy(
            src_ref=src, dst_ref=dst, send_sem=send_sem, recv_sem=recv_sem,
            device_id=to, device_id_type=MESH)

    def load(i, t):
        return pltpu.make_async_copy(
            factor_ref.at[i, core * tiles + t], raw.at[2 * core + i, t], load_sem.at[i, t])

    def part_out(i, t):
        return remote(factor_ref.at[i, other * tiles + t], raw.at[2 * core + i, t],
                      part_send.at[i, t], part_recv.at[i, t], partner)

    def mid_edge(i, target):
        src = factor_ref.at[i, tiles - target, 2 * target]
        return src, edge_raw.at[2 * core + i, 1 - target]

    def mid_out(i):
        src, dst = mid_edge(i, other)
        return remote(src, dst, mid_send.at[i], mid_recv.at[i], partner)

    def mid_own(i):
        src, dst = mid_edge(i, core)
        return pltpu.make_async_copy(src, dst, mid_self.at[i])

    def beside(side):
        return (2 * pair, l + 1) if side == 0 else (2 * pair + 1, l - 1)

    def edge_out(i, side):
        t, j = (2 * tiles - 1, 2) if side == 0 else (0, 0)
        return remote(factor_ref.at[i, t, j], edge_raw.at[2 * core + i, side],
                      edge_send.at[i, side], edge_recv.at[2 * core + i], beside(side))

    def edge_in(k):
        return remote(edge_raw.at[k, core], edge_raw.at[k, core],
                      edge_send.at[0, 0], edge_recv.at[k], partner)

    def strip_cut(ref, target):
        return ref.at[..., pl.ds(pl.multiple_of(target * (tiles - 1) * tile, tile), cells + tile)]

    def strip_slot(ref, target):
        return ref.at[core, ..., pl.ds(pl.multiple_of((1 - target) * tile, tile), cells + tile)]

    inputs = ((rhs_hbm, rhs), (couple_hbm, couple))

    def strip_out(n):
        src, dst = inputs[n]
        return remote(strip_cut(src, other), strip_slot(dst, other), strip_send.at[n], strip_recv.at[n], partner)

    def strip_own(n):
        src, dst = inputs[n]
        return pltpu.make_async_copy(strip_cut(src, core), strip_slot(dst, core), self_sem.at[n])

    def halo_out(n, side):
        src, dst = inputs[n]
        cut = pl.ds((2 * tiles - 1) * tile, tile) if side == 0 else pl.ds(0, tile)
        slot = pl.ds(0, tile) if side == 0 else pl.ds(cells + tile, tile)
        return remote(src.at[..., cut], dst.at[core, ..., slot],
                      halo_send.at[n, side], halo_recv.at[n, core], beside(side))

    def halo_in(n, owner):
        dst = inputs[n][1]
        slot = dst.at[owner, ..., pl.ds(pl.multiple_of(core * (cells + tile), tile), tile)]
        return remote(slot, slot, halo_send.at[n, 0], halo_recv.at[n, owner], partner)

    sends = (l < lat_count - 1, l > 0)
    outer = ((core == 0) & (l > 0)) | ((core == 1) & (l < lat_count - 1))

    small = [pltpu.make_async_copy(cell_hbm, cell_ref, small_sem.at[0]),
             pltpu.make_async_copy(layer_hbm, layer_ref, small_sem.at[1])]
    for copy in small:
        copy.start()
    for n in range(2):
        strip_own(n).start()
    for i in range(2):
        mid_own(i).start()
    for i in range(2):
        for t in range(tiles):
            load(i, t).start()

    for ref in (main_in, left_in, right_in, side_left, side_right, extra_left, extra_right):
        ref[...] = jnp.zeros_like(ref)

    @pl.when(jnp.logical_not(has_left))
    def _():
        edge_raw[:, 0] = jnp.zeros_like(edge_raw[:, 0])
        rhs[..., pl.ds(0, tile)] = jnp.zeros((2, 2, 2, shots, tile), F32)
        couple[..., pl.ds(0, tile)] = jnp.zeros((2, 2, 2, 2, tile), F32)

    @pl.when(jnp.logical_not(has_right))
    def _():
        edge_raw[:, 1] = jnp.zeros_like(edge_raw[:, 1])
        rhs[..., pl.ds(cells + tile, tile)] = jnp.zeros((2, 2, 2, shots, tile), F32)
        couple[..., pl.ds(cells + tile, tile)] = jnp.zeros((2, 2, 2, 2, tile), F32)

    barrier = pltpu.get_barrier_semaphore()
    steps = [(a, b) for a in (-1, 0, 1) for b in (-1, 0, 1) if (a, b) != (0, 0)] + [(0, -2), (0, 2)]
    peers = 0
    for a, b in steps:
        there = (pair + a >= 0) & (pair + a < pairs) & (half + b >= 0) & (half + b < halves)
        peers = peers + there.astype(jnp.int32)

        @pl.when(there)
        def _():
            pl.semaphore_signal(barrier, inc=1, device_id=place(a, b), device_id_type=MESH)
    pl.semaphore_wait(barrier, peers)

    for n in range(2):
        strip_out(n).start()
    for side in range(2):
        @pl.when(sends[side])
        def _():
            for n in range(2):
                halo_out(n, side).start()
    for i in (1, 0):
        mid_out(i).start()
        for side in range(2):
            @pl.when(sends[side])
            def _():
                edge_out(i, side).start()
    for i in range(2):
        for t in range(tiles):
            part_out(i, t).start()

    def convert(k):
        owner, i = k // 2, k % 2

        def step(t, carry):
            @pl.when(core == owner)
            def _():
                load(i, t).wait()

            @pl.when(core != owner)
            def _():
                remote(raw.at[k, t], raw.at[k, t], part_send.at[i, t], part_recv.at[i, t], partner).wait_recv()
            for j in range(3):
                for c in range(2):
                    high, low = split(raw[k, t, j, c])
                    weights[k, t, pl.ds(j * tile, tile), pl.ds(c * tile, tile)] = high
                    weights[k, t, pl.ds((3 + j) * tile, tile), pl.ds(c * tile, tile)] = low
            return carry
        lax.fori_loop(0, tiles, step, 0)

    def convert_edge(k):
        owner, i = k // 2, k % 2

        @pl.when(core == owner)
        def _():
            mid_own(i).wait()

        @pl.when(core != owner)
        def _():
            slot = edge_raw.at[k, other]
            remote(slot, slot, mid_send.at[i], mid_recv.at[i], partner).wait_recv()
        pl.when(outer)(edge_in(k).wait_recv)
        for side in range(2):
            for c in range(2):
                high, low = split(edge_raw[k, side, c])
                edge_weights[k, side, pl.ds(0, tile), pl.ds(c * tile, tile)] = high
                edge_weights[k, side, pl.ds(tile, tile), pl.ds(c * tile, tile)] = low

    convert(0)
    convert(1)
    for copy in small:
        copy.wait()
    for n in range(2):
        strip_own(n).wait()
        src, dst = inputs[n]
        slot = dst.at[other, ..., pl.ds(pl.multiple_of(other * tile, tile), cells + tile)]
        remote(slot, slot, strip_send.at[n], strip_recv.at[n], partner).wait_recv()

        @pl.when(outer)
        def _():
            for owner in range(2):
                halo_in(n, owner).wait_recv()

    row = lax.broadcasted_iota(jnp.int32, (shots, wide), 0)
    lane = lax.broadcasted_iota(jnp.int32, (shots, wide), 1) + (half * cells - tile)
    src_cell = jnp.zeros((shots, wide), jnp.int32)
    src_layer = jnp.zeros((shots, wide), jnp.int32)
    for s in range(shots):
        src_cell = jnp.where(row == s, cell_ref[s], src_cell)
        src_layer = jnp.where(row == s, layer_ref[s], src_layer)
    for k in range(4):
        hit = (src_layer == pair * 4 + k) & (src_cell == lane)
        rhs[k // 2, 0, k % 2] = rhs[k // 2, 0, k % 2] + jnp.where(hit, 4.0, 0.0).astype(F32)
    convert_edge(1)

    def put(target, at, parts):
        for c, value in enumerate(parts):
            high, low = split(value)
            target[pl.ds(c * shots, shots), at] = high
            target[pl.ds((2 + c) * shots, shots), at] = low

    def scaled(way, k, at, parts):
        real_coef = couple[k // 2, way, 0, k % 2:k % 2 + 1, at]
        imag_coef = couple[k // 2, way, 1, k % 2:k % 2 + 1, at]
        real_part = real_coef * parts[0] - imag_coef * parts[1]
        imag_part = real_coef * parts[1] + imag_coef * parts[0]
        if way == DOWN:
            real_part = rhs[k // 2, 0, k % 2, :, at] + real_part
            imag_part = rhs[k // 2, 1, k % 2, :, at] + imag_part
        return real_part, imag_part

    def product(value, right_side):
        both = jnp.dot(jnp.concatenate([value, value], axis=1), right_side, preferred_element_type=F32)
        both = both[: 2 * shots] + both[2 * shots:]
        return (both[:shots, :tile] - both[shots:, tile:], both[:shots, tile:] + both[shots:, :tile])

    def row_block(from_ref, k, t):
        return product(from_ref[:, pl.ds(t * tile, 3 * tile)], weights[k, t])

    def arrived(main, low, high, block):
        at = pl.ds(block * tile, tile)
        parts = []
        for c in range(2):
            value = main[c, :, at]
            if block < 2:
                value = value + low[c, :, at]
            if block >= tiles:
                value = value + high[c, :, pl.ds((block - tiles) * tile, tile)]
            parts.append(value)
        return parts

    blocks = tiles + 2
    chunks = [(0, 2), (blocks - 2, blocks), (2, blocks - 2)]

    def span(first, last):
        return pl.ds(first * tile, (last - first) * tile)

    def side_copies(way):
        out = out_ext.at[2 * way]
        return [
            (remote(out.at[:, :, span(0, 2)], side_right.at[way], side_send.at[way, 0], side_recv.at[way, 0],
                    place(0, -1)), has_left, has_right),
            (remote(out.at[:, :, span(tiles, blocks)], side_left.at[way], side_send.at[way, 1], side_recv.at[way, 1],
                    place(0, 1)), has_right, has_left),
        ]

    def hop_copies(way):
        out = out_ext.at[2 * way + 1]
        step = 1 if way == DOWN else -1
        onward = has_below if way == DOWN else has_above
        behind = has_above if way == DOWN else has_below
        table = [
            (span(0, 2), right_in.at[way], place(step, -1), onward & has_left, behind & has_right),
            (span(tiles, blocks), left_in.at[way], place(step, 1), onward & has_right, behind & has_left),
        ]
        for first, last in chunks:
            table.append((span(first, last), main_in.at[way, :, :, span(first, last)], place(step, 0), onward, behind))
        table.append((span(blocks - 1, blocks), extra_left.at[way], place(0, 1), has_right, has_left))
        table.append((span(0, 1), extra_right.at[way], place(0, -1), has_left, has_right))
        return [
            (remote(out.at[:, :, cut], dst, hop_send.at[way, num], hop_recv.at[way, num], to), go, come)
            for num, (cut, dst, to, go, come) in enumerate(table)
        ]

    zero = jnp.zeros((4 * shots, tile), BF16)
    inner[:, pl.ds(0, tile)] = zero
    inner[:, pl.ds(cells + tile, tile)] = zero

    def column_step(stage, k, base):
        for side in range(2):
            block = 0 if side == 0 else tiles + 1
            own = pl.ds(tile, tile) if side == 0 else pl.ds(cells, tile)
            real_part, imag_part = product(inner[:, own], edge_weights[k, side])
            out_ext[stage, 0, :, pl.ds(block * tile, tile)] = real_part
            out_ext[stage, 1, :, pl.ds(block * tile, tile)] = imag_part
        way = stage // 2
        copies = side_copies(way) if stage % 2 == 0 else hop_copies(way)
        starts = {tiles - 1: (0, 1)} if stage % 2 == 0 else {tiles - 1: (0, 1, 2, 3), tiles - 2: (4, 5, 6)}
        for t in [0, tiles - 1] + list(range(1, tiles - 1)):
            parts = row_block(inner, k, t)
            for c in range(2):
                value = parts[c]
                if base is not None:
                    value = value + base[k, c, :, pl.ds(t * tile, tile)]
                out_ext[stage, c, :, pl.ds((t + 1) * tile, tile)] = value
            for num in starts.get(t, ()):
                copy, go, _ = copies[num]
                pl.when(go)(copy.start)

    def take(copies):
        for copy, _, come in copies:
            pl.when(come)(copy.wait_recv)

    def first_source(way, k, main, low, high, result, result_k):
        for block in range(blocks):
            at = pl.ds(block * tile, tile)
            parts = arrived(main, low, high, block)
            if result is not None and 0 < block <= tiles:
                for c in range(2):
                    result[result_k, c, :, pl.ds((block - 1) * tile, tile)] = parts[c]
            put(source, at, scaled(way, k, at, parts))

    def second_source(way, row_k, k, result, base):
        for t in range(tiles):
            at = pl.ds(t * tile, tile)
            parts = row_block(source, row_k, t)
            if base is not None:
                parts = [parts[c] + base[row_k, c, :, at] for c in range(2)]
            for c in range(2):
                result[row_k, c, :, at] = parts[c]
            to = pl.ds((t + 1) * tile, tile)
            put(inner, to, scaled(way, k, to, parts))

    def total(way, result, k):
        take(hop_copies(way)[5:])
        out = out_ext.at[2 * way + 1]
        for c in range(2):
            for t in range(tiles):
                value = out[c, :, pl.ds((t + 1) * tile, tile)]
                if t == 0:
                    value = value + extra_left[way, c]
                if t == tiles - 1:
                    value = value + extra_right[way, c]
                result[k, c, :, pl.ds(t * tile, tile)] = value

    def second_layers():
        convert(2)
        convert(3)
        convert_edge(3)

    pl.when(has_above)(second_layers)
    take(hop_copies(DOWN)[:5])
    first_source(DOWN, 0, main_in.at[DOWN], left_in.at[DOWN], right_in.at[DOWN], None, 0)
    second_source(DOWN, 0, 1, waves, None)
    column_step(0, 1, None)
    pl.when(jnp.logical_not(has_above))(second_layers)
    take(side_copies(DOWN))
    first_source(DOWN, 2, out_ext.at[0], side_left.at[DOWN], side_right.at[DOWN], waves, 1)
    second_source(DOWN, 2, 3, waves, None)
    column_step(1, 3, None)
    convert_edge(2)
    convert_edge(0)
    total(DOWN, waves, 3)

    def result_copy(n, ref):
        return remote(ref.at[pl.ds(2 * other, 2)], result_in.at[n], result_send.at[n], result_recv.at[n], partner)

    result_copy(0, waves).start()

    @pl.when(jnp.logical_not(has_below))
    def _():
        for t in range(tiles):
            at = pl.ds(t * tile, tile)
            to = pl.ds((t + 1) * tile, tile)
            parts = [waves[3, c, :, at] for c in range(2)]
            for c in range(2):
                field[3, c, :, at] = parts[c]
            put(inner, to, scaled(UP, 2, to, parts))

    @pl.when(has_below)
    def _():
        take(hop_copies(UP)[:5])
        first_source(UP, 3, main_in.at[UP], left_in.at[UP], right_in.at[UP], None, 0)
        second_source(UP, 3, 2, field, waves)

    column_step(2, 2, waves)
    take(side_copies(UP))
    first_source(UP, 1, out_ext.at[2], side_left.at[UP], side_right.at[UP], field, 2)
    second_source(UP, 1, 0, field, waves)
    column_step(3, 0, waves)
    total(UP, field, 0)
    result_copy(1, field).start()

    for n, (ref, out_ref) in enumerate(((waves, waves_ref), (field, field_ref))):
        mine = pl.ds(pl.multiple_of(core * cells, tile), cells)
        theirs = pl.ds(pl.multiple_of(other * cells, tile), cells)
        for i in range(2):
            for c in range(2):
                out_ref[c, i, :, mine] = ref[2 * core + i, c]
        result_copy(n, ref).wait_recv()
        for i in range(2):
            for c in range(2):
                out_ref[c, i, :, theirs] = result_in[n, i, c]

    for n, ref in enumerate((waves, field)):
        result_copy(n, ref).wait_send()
        strip_out(n).wait_send()
    for i in range(2):
        mid_out(i).wait_send()
        for t in range(tiles):
            part_out(i, t).wait_send()
    for side in range(2):
        @pl.when(sends[side])
        def _():
            for n in range(2):
                halo_out(n, side).wait_send()
                edge_out(n, side).wait_send()
    for way in (DOWN, UP):
        for copy, go, _ in side_copies(way) + hop_copies(way):
            pl.when(go)(copy.wait_send)


def shards(depth_count, lat_count, rhs_field, src_cell, src_layer, factor, couple):
    layers, full_tiles = factor.shape[:2]
    tile = factor.shape[-1]
    shots = rhs_field.shape[2]
    assert layers == 2 and full_tiles % 2 == 0 and depth_count % 2 == 0
    tiles = full_tiles // 2
    cells = tiles * tile
    wide = cells + 2 * tile
    vmem = pl.BlockSpec(memory_space=pltpu.VMEM)
    dma = pltpu.SemaphoreType.DMA
    return pl.pallas_call(
        functools.partial(kernel, depth_count, lat_count),
        out_shape=[jax.ShapeDtypeStruct(rhs_field.shape, F32)] * 2,
        in_specs=[pl.BlockSpec(memory_space=pltpu.HBM)] * 5,
        out_specs=[vmem, vmem],
        scratch_shapes=[
            pltpu.SMEM(src_cell.shape, jnp.int32),
            pltpu.SMEM(src_layer.shape, jnp.int32),
            pltpu.VMEM((2, 2, 2, shots, wide), F32),
            pltpu.VMEM((2, 2, 2, 2, wide), F32),
            pltpu.VMEM((4, tiles, 3, 2, tile, tile), F32),
            pltpu.VMEM((4, tiles, 6 * tile, 2 * tile), BF16),
            pltpu.VMEM((4, 2, 2, tile, tile), F32),
            pltpu.VMEM((4, 2, 2 * tile, 2 * tile), BF16),
            pltpu.VMEM((4 * shots, wide), BF16),
            pltpu.VMEM((4 * shots, wide), BF16),
            pltpu.VMEM((4, 2, shots, wide), F32),
            pltpu.VMEM((2, 2, shots, wide), F32),
            *[pltpu.VMEM((2, 2, shots, 2 * tile), F32)] * 4,
            *[pltpu.VMEM((2, 2, shots, tile), F32)] * 2,
            *[pltpu.VMEM((4, 2, shots, cells), F32)] * 2,
            pltpu.VMEM((2, 2, 2, shots, cells), F32),
            dma((2,)), dma((2,)), dma((2, tiles)), dma((2, tiles)), dma((2, tiles)),
            dma((2,)), dma((2,)), dma((2,)),
            dma((2, 2)), dma((4,)), dma((2,)), dma((2,)), dma((2, 2)), dma((2, 2)),
            dma((2, 7)), dma((2, 7)), dma((2, 2)), dma((2, 2)), dma((2,)), dma((2,)),
        ],
        compiler_params=pltpu.CompilerParams(
            collective_id=0, has_side_effects=True, vmem_limit_bytes=63 * 1024 * 1024),
        name="sweeps",
    )(src_cell, src_layer, rhs_field, couple, factor)


def solution(mesh):
    placed = (
        P(None, "depth", None, "lat"),
        P(),
        P(),
        P("depth", "lat", None, None, None, None),
        P(None, None, "depth", "lat"),
    )
    return jax.shard_map(
        functools.partial(shards, mesh.shape["depth"], mesh.shape["lat"]),
        mesh=mesh,
        in_specs=placed,
        out_specs=(P(None, "depth", None, "lat"), P(None, "depth", None, "lat")),
        check_vma=False,
    )
```

time: 563 us -> 69.5 us (0.12); the launches traced: 553 us -> 69.3 us
  starting transfers between devices: 194 us -> 0 us
  matrix products: 128 us -> 0 us
  waiting for transfers between devices: 115 us -> 0 us
  local copies, waits for them, and re-layouts: 88.1 us -> 3.14 us
  Pallas kernels: 0 us -> 65.5 us
  other arithmetic: 23.1 us -> 0 us
    ppermute x80 -> x0, starting transfers between devices: 194 us -> none  [the longest x32 112 us: extended(): lax.ppermute(lax.slice_in_dim(block, block.shape[dim] - width, None, axis...]
    dot_general x128 -> x0, matrix products: 128 us -> none  [the longest x32 32.2 us: block_product(): jnp.einsum(form, shifted[1], blocks[:, :, 0], precision=high)]
    ppermute x80 -> x0, waiting for transfers between devices: 115 us -> none  [the longest x32 75.9 us: extended(): lax.ppermute(lax.slice_in_dim(block, 0, width, axis=dim), axis, backward)]
    squeeze x25 -> x0, local copies, waits for them, and re-layouts: 68.3 us -> none  [the longest x8 26.2 us: ascend(): factor[layer_num]]
    pallas_call x0 -> x1, Pallas kernels: none -> 65.5 us  [shards(): pl.pallas_call(functools.partial(kernel, depth_count, lat_count), out_sha...]
    reshape x32 -> x0, other arithmetic: 11.8 us -> none  [block_product(): jnp.stack([padded[:, :, offset * tile_cells:offset * tile_cells + strip_c...]
    slice x32 -> x0, local copies, waits for them, and re-layouts: 11.2 us -> none  [the longest x16 6.42 us: complex_scale(): real_part = coef[0][None, :] * vector[0] - coef[1][None, :] * vector[1]]
    sub x24 -> x0, other arithmetic: 6.52 us -> none  [complex_scale(): real_part = coef[0][None, :] * vector[0] - coef[1][None, :] * vector[1]]
  transfers between devices with their start and end apart: 80 -> 0, of which waited for: 40 -> 0; matrix products, arithmetic and copies ran while one was open for 12% -> 0% of each run, Pallas kernels for 0% -> 0%
where the time goes in v3:
time: 69.5 us; the launch traced here: 69.3 us
  Pallas kernels  65.5 us (94%)
  local copies, waits for them, and re-layouts  3.14 us (5%)
    pallas_call x1, Pallas kernels, shards(): pl.pallas_call(functools.partial(kernel, depth_count, lat_count), out_sha...  65.5 us
    unnamed x2, local copies, waits for them, and re-layouts  3.14 us

profile of v3, /device:TPU:0, one launch (start us, length us, event | category | flops | bytes accessed | tf_op | source)
XLA Modules:
  0.0 69.3 jit_solution(14119277623312627253)
XLA Ops:
  0.6 65.5 %sweeps.1 = (f32[2,2,8,1024]{3,2,1,0:T(8,128)}, f32[2,2,8,1024]{3,2,1,0:T(8,128)}) custom-call(s32[8]{0:T(128)} %cell_hbm.1, s32[8]{0:T(128)} %layer_hbm.1, f32[2,2,8,1024]{3,2,1,0:T(8,128)} %rhs_hbm.1, f32[2,2,2,1024]{3,2,1,0:T(2,128)} %couple_hbm.1, f32[2,8,3,2,128,128]{5,4,3,2,1,0:T(8,128)} %factor_ref.1), custom_call_target="tpu_custom_call" | custom-call | tf_op jit(solution)/shard_map/sweeps/pallas_call | solution.py:457
  66.2 1.6 %copy.9 = f32[2,2,8,1024]{3,2,1,0:T(8,128)} copy(f32[2,2,8,1024]{3,2,1,0:T(8,128)} %get-tuple-element.4) | data formatting | bytes 262144
  67.7 1.6 %copy.10 = f32[2,2,8,1024]{3,2,1,0:T(8,128)} copy(f32[2,2,8,1024]{3,2,1,0:T(8,128)} %get-tuple-element.5) | data formatting | bytes 262144

commit v4 on v3

--- a/solution.py
+++ b/solution.py
@@ -238,10 +238,9 @@
     convert_edge(1)
 
     def put(target, at, parts):
-        for c, value in enumerate(parts):
-            high, low = split(value)
-            target[pl.ds(c * shots, shots), at] = high
-            target[pl.ds((2 + c) * shots, shots), at] = low
+        high, low = split(jnp.concatenate(parts, axis=0))
+        target[pl.ds(0, 2 * shots), at] = high
+        target[pl.ds(2 * shots, 2 * shots), at] = low
 
     def scaled(way, k, at, parts):
         real_coef = couple[k // 2, way, 0, k % 2:k % 2 + 1, at]
@@ -482,9 +481,10 @@
             dma((2, 7)), dma((2, 7)), dma((2, 2)), dma((2, 2)), dma((2,)), dma((2,)),
         ],
         compiler_params=pltpu.CompilerParams(
-            collective_id=0, has_side_effects=True, vmem_limit_bytes=63 * 1024 * 1024),
+            collective_id=0, has_side_effects=True, vmem_limit_bytes=44 * 1024 * 1024),
         name="sweeps",
-    )(src_cell, src_layer, rhs_field, couple, factor)
+    )(*[pltpu.with_memory_space_constraint(value, pltpu.HBM)
+        for value in (src_cell, src_layer, rhs_field, couple, factor)])
 
 
 def solution(mesh):

time: 69.5 us -> 66.9 us (0.963)
  local copies, waits for them, and re-layouts: 3.14 us -> 1.31 us
    unnamed x2, local copies, waits for them, and re-layouts: 3.14 us -> 1.31 us
where the time goes in v4:
time: 66.9 us; the launch traced here: 66.8 us
  Pallas kernels  64.9 us (97%)
  local copies, waits for them, and re-layouts  1.31 us (2%)
    pallas_call x1, Pallas kernels, shards(): pl.pallas_call(functools.partial(kernel, depth_count, lat_count), out_sha...  64.9 us

profile of v4, /device:TPU:0, one launch (start us, length us, event | category | flops | bytes accessed | tf_op | source)
XLA Modules:
  0.0 66.8 jit_solution(18064402113785784007)
XLA Ops:
  0.6 64.9 %sweeps.1 = (f32[2,2,8,1024]{3,2,1,0:T(8,128)S(1)}, f32[2,2,8,1024]{3,2,1,0:T(8,128)S(1)}) custom-call(s32[8]{0:T(128)} %cell_hbm.1, s32[8]{0:T(128)} %layer_hbm.1, f32[2,2,8,1024]{3,2,1,0:T(8,128)} %rhs_hbm.1, f32[2,2,2,1024]{3,2,1,0:T(2,128)} %couple_hbm.1, f32[2,8,3,2,128,128]{5,4,3,2,1,0:T(8,128)} %factor_ref.1), custom_call_target="tpu_custom_call" | custom-call | tf_op jit(solution)/shard_map/sweeps/pallas_call | solution.py:456
  65.5 0.7 copy.9
  66.1 0.7 copy.10

commit v5 on v4

--- a/solution.py
+++ b/solution.py
@@ -273,7 +273,7 @@
         return parts
 
     blocks = tiles + 2
-    chunks = [(0, 2), (blocks - 2, blocks), (2, blocks - 2)]
+    chunks = [(0, blocks)]
 
     def span(first, last):
         return pl.ds(first * tile, (last - first) * tile)
@@ -318,7 +318,7 @@
             out_ext[stage, 1, :, pl.ds(block * tile, tile)] = imag_part
         way = stage // 2
         copies = side_copies(way) if stage % 2 == 0 else hop_copies(way)
-        starts = {tiles - 1: (0, 1)} if stage % 2 == 0 else {tiles - 1: (0, 1, 2, 3), tiles - 2: (4, 5, 6)}
+        starts = {tiles - 1: (0, 1)} if stage % 2 == 0 else {tiles - 1: (0, 1), tiles - 2: (2, 3, 4)}
         for t in [0, tiles - 1] + list(range(1, tiles - 1)):
             parts = row_block(inner, k, t)
             for c in range(2):
@@ -355,7 +355,7 @@
             put(inner, to, scaled(way, k, to, parts))
 
     def total(way, result, k):
-        take(hop_copies(way)[5:])
+        take(hop_copies(way)[3:])
         out = out_ext.at[2 * way + 1]
         for c in range(2):
             for t in range(tiles):
@@ -372,7 +372,7 @@
         convert_edge(3)
 
     pl.when(has_above)(second_layers)
-    take(hop_copies(DOWN)[:5])
+    take(hop_copies(DOWN)[:3])
     first_source(DOWN, 0, main_in.at[DOWN], left_in.at[DOWN], right_in.at[DOWN], None, 0)
     second_source(DOWN, 0, 1, waves, None)
     column_step(0, 1, None)
@@ -402,7 +402,7 @@
 
     @pl.when(has_below)
     def _():
-        take(hop_copies(UP)[:5])
+        take(hop_copies(UP)[:3])
         first_source(UP, 3, main_in.at[UP], left_in.at[UP], right_in.at[UP], None, 0)
         second_source(UP, 3, 2, field, waves)
 
@@ -478,7 +478,7 @@
             dma((2,)), dma((2,)), dma((2, tiles)), dma((2, tiles)), dma((2, tiles)),
             dma((2,)), dma((2,)), dma((2,)),
             dma((2, 2)), dma((4,)), dma((2,)), dma((2,)), dma((2, 2)), dma((2, 2)),
-            dma((2, 7)), dma((2, 7)), dma((2, 2)), dma((2, 2)), dma((2,)), dma((2,)),
+            dma((2, 5)), dma((2, 5)), dma((2, 2)), dma((2, 2)), dma((2,)), dma((2,)),
         ],
         compiler_params=pltpu.CompilerParams(
             collective_id=0, has_side_effects=True, vmem_limit_bytes=44 * 1024 * 1024),

time: 66.9 us -> 67.1 us (level)
  no operation moved by 1% of the time
where the time goes in v5:
time: 67.1 us; the launch traced here: 67 us
  Pallas kernels  65 us (97%)
  local copies, waits for them, and re-layouts  1.31 us (2%)
    pallas_call x1, Pallas kernels, shards(): pl.pallas_call(functools.partial(kernel, depth_count, lat_count), out_sha...  65 us

profile of v5, /device:TPU:0, one launch (start us, length us, event | category | flops | bytes accessed | tf_op | source)
XLA Modules:
  0.0 67.0 jit_solution(10631506268672492676)
XLA Ops:
  0.6 65.0 %sweeps.1 = (f32[2,2,8,1024]{3,2,1,0:T(8,128)S(1)}, f32[2,2,8,1024]{3,2,1,0:T(8,128)S(1)}) custom-call(s32[8]{0:T(128)} %cell_hbm.1, s32[8]{0:T(128)} %layer_hbm.1, f32[2,2,8,1024]{3,2,1,0:T(8,128)} %rhs_hbm.1, f32[2,2,2,1024]{3,2,1,0:T(2,128)} %couple_hbm.1, f32[2,8,3,2,128,128]{5,4,3,2,1,0:T(8,128)} %factor_ref.1), custom_call_target="tpu_custom_call" | custom-call | tf_op jit(solution)/shard_map/sweeps/pallas_call | solution.py:456
  65.7 0.7 copy.9
  66.3 0.7 copy.10
